TPU v7x, 32 devices: a whole 2x2x4 slice. The times are simulated.
32 devices in a mesh: groups: 2 (over x), band: 16 (over z, y, core).
Axes of the slice: x: 2, y: 2, z: 4, core: 2. Of those that a mesh axis runs over, the one named last changes fastest.
Arguments:
- state: float32 [83, 65536], P(None, ('groups', 'band')), parts along dimension 1, may hold values from -36 to 36
- mesh_latent: bfloat16 [65536, 512], P(('groups', 'band')), parts along dimension 0, may hold values from -6 to 6
- m2g_src: int32 [65536, 3], P(('groups', 'band')), parts along dimension 0, may hold values from 0 to 32767, as said below
- g2m_owner: int32 [65536, 1], P(('groups', 'band')), parts along dimension 0, may hold values from 0 to 15, as said below
- g2m_node: int32 [65536, 1], P(('groups', 'band')), parts along dimension 0, may hold values from 0 to 2047
- mesh_src: int32 [65536, 6], P(('groups', 'band')), parts along dimension 0, may hold values from 0 to 32767, as said below
- norm_gain: float32 [83], replicated, may hold values from 0.1 to 1.9
- w_dec_mesh: bfloat16 [512, 512], replicated, may hold values from -0.25 to 0.25
- w_dec_grid: bfloat16 [83, 512], replicated, may hold values from -0.625 to 0.625
- w_dec_out: bfloat16 [512, 83], replicated, may hold values from -0.15625 to 0.15625
- w_enc: bfloat16 [83, 512], replicated, may hold values from -0.625 to 0.625
- w_enc_out: bfloat16 [512, 512], replicated, may hold values from -0.125 to 0.125
- w_proc_src: bfloat16 [512, 512], replicated, may hold values from -0.25 to 0.25
- w_proc_dst: bfloat16 [512, 512], replicated, may hold values from -0.25 to 0.25
- w_proc_out: bfloat16 [512, 512], replicated, may hold values from -0.109375 to 0.109375
Outputs:
- new_state: float32 [83, 65536], P(None, ('groups', 'band')), parts along dimension 1
- mesh_out: bfloat16 [65536, 512], P(('groups', 'band')), parts along dimension 0
There are 2 independent parts, one for each index of `groups`. A program takes and returns all parts, laid end to end along the dimension named above; an argument that names none is the same for every part. Nothing has to cross between parts.
Inputs may be any that keep to these rules, and one draw needn't show every extreme that they name: `m2g_src`: grid point g lies in band b = g // 2048; its senders lie from b * 2048 - 128 to (b + 1) * 2048 + 127, clipped to the mesh, and both ends are named in every band. `mesh_src`: mesh node m lies in patch b = m // 2048; its senders lie from b * 2048 - 128 to (b + 1) * 2048 + 127, clipped to the mesh, and both ends are named in every patch. `g2m_owner`: A grid point of band b names patch b, b - 1 or b + 1. Rows naming b - 1 lie among the band's first 256 rows, rows naming b + 1 among its last 256; each neighbour is named at most 128 times by one band, and exactly 128 times by every band of the first and last eighth of the bands (at least one band at each end) for each neighbour it has.
All inputs are finite; a program needn't handle non-finite values.
Results may differ from a plain program's by a relative error of at most 0.0056.
Values may be sent and summed in bfloat16 or wider, within the bound.
A program may use at most 128 MiB of HBM per device.

v0:
```python
import jax
import jax.numpy as jnp
from jax import lax
from jax.sharding import PartitionSpec as P

HALO = 128
KD = 3
KN = 6


def extended(cells, sides, width):
    for axis, dim in sides:
        count = lax.axis_size(axis)
        ends = count - 1
        head = lax.slice_in_dim(cells, 0, width, axis=dim)
        tail = lax.slice_in_dim(cells, cells.shape[dim] - width, cells.shape[dim], axis=dim)
        cells = jnp.concatenate(
            [
                lax.ppermute(tail, axis, [(i, (i + 1) % count) for i in range(ends)]),
                cells,
                lax.ppermute(head, axis, [((i + 1) % count, i) for i in range(ends)]),
            ],
            axis=dim,
        )
    return cells


def contract_first(left, right):
    return lax.dot_general(
        left, right, (((0,), (0,)), ((), ())), preferred_element_type=jnp.float32
    )


def silu_sum(source_table, positions, baseline, fanout):
    row_count = positions.shape[0]
    picked_all = jnp.take(source_table, positions.reshape(-1), axis=0).reshape(
        row_count, fanout, source_table.shape[1]
    )
    summed = jnp.zeros(baseline.shape, jnp.float32)
    for neighbour in range(fanout):
        summed = summed + jax.nn.silu(picked_all[:, neighbour].astype(jnp.float32) + baseline)
    return summed


def sum_into_nodes(node_ids, rows, node_count):
    return jax.ops.segment_sum(rows.astype(jnp.float32), node_ids, num_segments=node_count)


def slot_table(flags, nodes, capacity, empty_id):
    width = flags.shape[0]
    row_range = jnp.arange(width, dtype=jnp.int32)
    earlier = row_range[None, :] < row_range[:, None]
    ranks = jnp.sum(jnp.where(earlier, flags[None, :], 0), axis=1)
    slot_range = jnp.arange(capacity, dtype=jnp.int32)
    chosen = (flags[None, :] == 1) & (ranks[None, :] == slot_range[:, None])
    picked = chosen.astype(jnp.int32)
    filled = jnp.sum(picked, axis=1)
    ids = jnp.sum(picked * nodes[None, :], axis=1) + (1 - filled) * empty_id
    return (chosen.astype(jnp.bfloat16), ids)


def shards(
    state,
    mesh_latent,
    m2g_src,
    g2m_owner,
    g2m_node,
    mesh_src,
    norm_gain,
    w_dec_mesh,
    w_dec_grid,
    w_dec_out,
    w_enc,
    w_enc_out,
    w_proc_src,
    w_proc_dst,
    w_proc_out,
):
    position = lax.axis_index("band")
    mesh_rows = mesh_latent.shape[0]
    grid_rows = state.shape[1]
    capacity = grid_rows // 16
    window = 2 * capacity
    offset_row = position * mesh_rows - HALO
    projected = jnp.dot(mesh_latent, w_dec_mesh, preferred_element_type=jnp.float32).astype(
        jnp.bfloat16
    )
    padded = extended(projected, (("band", 0),), HALO)
    grid_half = state.astype(jnp.bfloat16)
    receiver = contract_first(grid_half, w_dec_grid)
    local_sources = m2g_src - offset_row
    decoded = silu_sum(padded, local_sources, receiver, KD).astype(jnp.bfloat16)
    update = lax.dot_general(
        w_dec_out, decoded, (((0,), (1,)), ((), ())), preferred_element_type=jnp.float32
    )
    new_state = state + update
    average = jnp.mean(new_state, axis=0, keepdims=True)
    centered = new_state - average
    variance = jnp.mean(centered * centered, axis=0, keepdims=True)
    normed = (centered * lax.rsqrt(variance + 1e-05) * norm_gain[:, None]).astype(jnp.bfloat16)
    relative = g2m_owner[:, 0] - position
    nodes = g2m_node[:, 0]
    lower_flags = (relative[:window] == -1).astype(jnp.int32)
    upper_flags = (relative[grid_rows - window :] == 1).astype(jnp.int32)
    lower_pick, lower_ids = slot_table(lower_flags, nodes[:window], capacity, mesh_rows)
    upper_pick, upper_ids = slot_table(
        upper_flags, nodes[grid_rows - window :], capacity, mesh_rows
    )
    node_ids = jnp.concatenate([lower_ids, upper_ids], axis=0)
    message_local = jax.nn.silu(contract_first(normed, w_enc)).astype(jnp.bfloat16)
    local_ids = jnp.where(relative == 0, nodes, mesh_rows)
    collected = sum_into_nodes(local_ids, message_local, mesh_rows)
    lower_rows = jnp.dot(lower_pick, message_local[:window], preferred_element_type=jnp.float32)
    upper_rows = jnp.dot(
        upper_pick, message_local[grid_rows - window :], preferred_element_type=jnp.float32
    )
    outbox = jnp.concatenate([lower_rows, upper_rows], axis=0).astype(jnp.bfloat16)
    arrived, arrived_ids = (
        extended(outbox, (("band", 0),), capacity),
        extended(node_ids, (("band", 0),), capacity),
    )
    message = jnp.concatenate([arrived[:capacity], arrived[3 * capacity :]], axis=0)
    rim_ids = jnp.concatenate([arrived_ids[:capacity], arrived_ids[3 * capacity :]], axis=0)
    collected = collected + sum_into_nodes(rim_ids.astype(jnp.int32), message, mesh_rows)
    encoded = collected.astype(jnp.bfloat16)
    mesh_mid = (
        mesh_latent.astype(jnp.float32)
        + jnp.dot(encoded, w_enc_out, preferred_element_type=jnp.float32)
    ).astype(jnp.bfloat16)
    sender = jnp.dot(mesh_mid, w_proc_src, preferred_element_type=jnp.float32).astype(jnp.bfloat16)
    sender_padded = extended(sender, (("band", 0),), HALO)
    own = jnp.dot(mesh_mid, w_proc_dst, preferred_element_type=jnp.float32)
    local_mesh = mesh_src - offset_row
    edges_sum = silu_sum(sender_padded, local_mesh, own, KN).astype(jnp.bfloat16)
    mesh_out = (
        mesh_mid.astype(jnp.float32)
        + jnp.dot(edges_sum, w_proc_out, preferred_element_type=jnp.float32)
    ).astype(jnp.bfloat16)
    return (new_state, mesh_out)


def solution(mesh):
    placed = (
        P(None, ("groups", "band")),
        P(("groups", "band"), None),
        P(("groups", "band"), None),
        P(("groups", "band"), None),
        P(("groups", "band"), None),
        P(("groups", "band"), None),
        P(),
        P(),
        P(),
        P(),
        P(),
        P(),
        P(),
        P(),
        P(),
    )
    return jax.shard_map(
        shards,
        mesh=mesh,
        in_specs=placed,
        out_specs=(P(None, ("groups", "band")), P(("groups", "band"), None)),
        check_vma=False,
    )
```

profile of v0, /device:TPU:1, one launch (start us, length us, event | category | flops | bytes accessed | tf_op | source)
XLA Modules:
  0.0 231.7 jit_solution(4457342547811226537)
XLA Ops:
  0.6 0.0 copy-start
  0.7 0.8 fusion.31
  1.4 0.7 compare_select_fusion.4
  2.2 0.1 select_reduce_fusion.1
  2.3 0.1 convert_reduce_fusion.1
  2.4 4.5 %collective-permute-start.2 = (s32[128]{0:T(128)S(1)}, s32[128]{0:T(128)S(1)}, u32[]{:S(2)}, u32[]{:S(2)}) collective-permute-start(s32[128]{0:T(128)S(1)} %multiply_add_fusion.1), channel_id=1, source_target_pairs={{0,1},{1,2},{2,3},{3,4},{4,5},{5,6},{6,7},{7,8},{8,9},{9,10},{10,1... | collective-permute-start | bytes 1544 | tf_op jit(solution)/shard_map/ppermute | solution.py:19
  7.0 0.1 select_reduce_fusion
  7.1 0.1 convert_reduce_fusion
  7.2 0.0 copy-start.10
  7.2 2.1 collective-permute-start.3
  9.3 2.8 %convolution_convert_fusion.1 = bf16[2048,512]{1,0:T(8,128)(2,1)S(1)} fusion(bf16[2048,512]{1,0:T(8,128)(2,1)} %param.16, bf16[512,512]{1,0:T(8,128)(2,1)S(1)} %copy-done), kind=kOutput, calls=%fused_computation.24 | convolution fusion | flops 1074790400 | bytes 4718592 | tf_op jit(solution)/shard_map/dot_general | solution.py:85
  12.2 1.3 copy-done.2
  13.5 3.6 %collective-permute-start = (bf16[128,512]{1,0:T(8,128)(2,1)S(1)}, bf16[128,512]{1,0:T(8,128)(2,1)S(1)}, u32[]{:S(2)}, u32[]{:S(2)}) collective-permute-start(bf16[128,512]{1,0:T(8,128)(2,1)S(1)} %get-tuple-element.14), channel_id=1, source_target_pairs={{0,1},{1,2},{2,3},{3,4},{4,5},{5,6},{6,7},{7,8},{8,9},{9,10},{10,1... | collective-permute-start | bytes 393224 | tf_op jit(solution)/shard_map/ppermute | solution.py:19
  17.2 1.9 collective-permute-start.1
  19.2 0.4 copy.23
  19.5 0.8 reshape.148
  20.4 0.4 copy.21
  20.7 0.7 reshape.147
  21.5 1.9 collective-permute-done.1
  23.4 1.7 pad_maximum_fusion
  25.2 25.5 %gather_fusion = bf16[6144,512]{1,0:T(8,128)(2,1)} fusion(bf16[2304,512]{1,0:T(8,128)(2,1)S(1)} %pad_maximum_fusion, s32[6144]{0:T(1024)S(1)} %broadcast_clamp_fusion.1), kind=kCustom, calls=%fused_computation | custom fusion | bytes 12607488 | tf_op jit(solution)/shard_map/jit(_take)/gather | solution.py:36
  50.7 16.8 %gather.13 = bf16[2048,3,512]{2,1,0:T(4,128)(2,1)} reshape(bf16[6144,512]{1,0:T(8,128)(2,1)} %gather_fusion) | data formatting | bytes 12582912 | tf_op jit(solution)/shard_map/jit(_take)/gather | solution.py:36
  67.5 9.5 %copy_select_fusion.1 = bf16[2048,3,512]{2,0,1:T(8,128)(2,1)} fusion(bf16[2048,3,512]{2,1,0:T(4,128)(2,1)} %gather.13, pred[2048,3]{0,1:T(4,128)(4,1)S(1)} %get-tuple-element.10), kind=kLoop, calls=%fused_computation.5 | loop fusion | flops 3145728 | bytes 12589056 | tf_op jit(solution)/shard_map/jit(_take)/select_n | solution.py:36
  77.1 0.0 copy-start.17
  77.1 7.0 %fusion.32 = (f32[2048]{0:T(1024)S(1)}, f32[83,2048]{1,0:T(8,128)S(1)}) fusion(f32[83,2048]{1,0:T(8,128)S(1)} %copy-done.11, bf16[512,83]{0,1:T(8,128)(2,1)S(1)} %copy-done.14, bf16[2048,3,512]{2,0,1:T(8,128)(2,1)} %copy_select_fusion.1, bf16[83,512]{1,0:T(8,128)(2,1)S(1)} %copy-done.15), kind=kOutput, calls=%fused_computation.97 | convolution fusion | flops 370655232 | bytes 8601600 | tf_op jit(solution)/shard_map/dot_general | solution.py:93
  84.1 0.0 copy-start.7
  84.1 0.1 multiply_reduce_fusion
  84.3 1.4 multiply_convert_fusion
  85.7 0.0 copy-start.6
  85.7 0.2 convolution_convert_fusion.2
  85.9 0.2 convolution_convert_fusion.3
  86.1 1.9 collective-permute-start.4
  88.0 2.6 %collective-permute-start.5 = (bf16[128,512]{1,0:T(8,128)(2,1)S(1)}, bf16[128,512]{1,0:T(8,128)(2,1)S(1)}, u32[]{:S(2)}, u32[]{:S(2)}) collective-permute-start(bf16[128,512]{1,0:T(8,128)(2,1)S(1)} %convolution_convert_fusion.2), channel_id=1, source_target_pairs={{1,0},{2,1},{3,2},{4,3},{5,4},{6,5},{7,6},{8,7},{9,8},{10,9},{11,1... | collective-permute-start | bytes 393224 | tf_op jit(solution)/shard_map/ppermute | solution.py:21
  90.6 0.1 compare_select_fusion
  90.7 15.6 %scatter_custom_fusion = f32[2048,512]{1,0:T(8,128)} fusion(s32[2048]{0:T(1024)S(1)} %bitcast.84, bf16[2048,512]{1,0:T(8,128)(2,1)} %copy-done.6, f32[]{:T(128)} %constant.64.clone.1), kind=kCustom, calls=%fused_computation.19 | custom fusion | flops 2097152 | bytes 6291460 | tf_op jit(solution)/shard_map/scatter-add | solution.py:46
  106.4 4.3 %scatter_custom_fusion.1 = f32[2048,512]{1,0:T(8,128)} fusion(s32[256]{0:T(256)S(1)} %pad_add_fusion, f32[]{:T(128)} %constant.64.clone.1, bf16[128,512]{1,0:T(8,128)(2,1)S(1)} %collective-permute-done.5, bf16[]{:T(256)} %constant.69, bf16[128,512]{1,0:T(8,128)(2,1)S(1)} %collective-permute-done.4), kind=kCustom, calls=%fused_computation.38 | custom fusion | flops 655360 | bytes 4456454 | tf_op jit(solution)/shard_map/scatter-add | solution.py:46
  110.7 4.8 %add_convert_fusion.2 = bf16[2048,512]{1,0:T(8,128)(2,1)S(1)} fusion(bf16[2048,512]{1,0:T(8,128)(2,1)S(1)} %copy-done.3, bf16[512,512]{1,0:T(8,128)(2,1)S(1)} %copy-done.8, f32[2048,512]{1,0:T(8,128)} %scatter_custom_fusion, f32[2048,512]{1,0:T(8,128)} %scatter_custom_fusion.1), kind=kOutput, calls=%fused_computation.17 | convolution fusion | flops 1078984704 | bytes 13107200 | tf_op jit(solution)/shard_map/dot_general | solution.py:128
  115.5 0.0 copy-start.4
  115.5 1.3 convolution_convert_fusion
  116.8 0.1 copy-done.4
  116.9 4.8 %collective-permute-start.6 = (bf16[128,512]{1,0:T(8,128)(2,1)S(1)}, bf16[128,512]{1,0:T(8,128)(2,1)S(1)}, u32[]{:S(2)}, u32[]{:S(2)}) collective-permute-start(bf16[128,512]{1,0:T(8,128)(2,1)S(1)} %get-tuple-element.12), channel_id=1, source_target_pairs={{0,1},{1,2},{2,3},{3,4},{4,5},{5,6},{6,7},{7,8},{8,9},{9,10},{10,1... | collective-permute-start | bytes 393224 | tf_op jit(solution)/shard_map/ppermute | solution.py:19
  121.7 2.1 collective-permute-start.7
  123.9 4.1 %collective-permute-done.7 = bf16[128,512]{1,0:T(8,128)(2,1)S(1)} collective-permute-done((bf16[128,512]{1,0:T(8,128)(2,1)S(1)}, bf16[128,512]{1,0:T(8,128)(2,1)S(1)}, u32[]{:S(2)}, u32[]{:S(2)}) %collective-permute-start.7) | collective-permute-done | bytes 131104 | tf_op jit(solution)/shard_map/ppermute | solution.py:21
  128.0 0.2 pad_maximum_fusion.1
  128.1 50.1 %gather_fusion.1 = bf16[12288,512]{1,0:T(8,128)(2,1)} fusion(bf16[2304,512]{1,0:T(8,128)(2,1)S(1)} %pad_maximum_fusion.1, s32[12288]{0:T(1024)S(1)} %broadcast_clamp_fusion), kind=kCustom, calls=%fused_computation.1 | custom fusion | bytes 25214976 | tf_op jit(solution)/shard_map/jit(_take)/gather | solution.py:36
  178.2 21.0 %gather.15 = bf16[2048,6,512]{2,1,0:T(8,128)(2,1)} reshape(bf16[12288,512]{1,0:T(8,128)(2,1)} %gather_fusion.1) | data formatting | bytes 25165824 | tf_op jit(solution)/shard_map/jit(_take)/gather | solution.py:36
  199.3 19.3 %copy_select_fusion = bf16[2048,6,512]{2,0,1:T(8,128)(2,1)} fusion(bf16[2048,6,512]{2,1,0:T(8,128)(2,1)} %gather.15, pred[2048,6]{0,1:T(8,128)(4,1)S(1)} %get-tuple-element.6), kind=kLoop, calls=%fused_computation.4 | loop fusion | flops 6291456 | bytes 25178112 | tf_op jit(solution)/shard_map/jit(_take)/select_n | solution.py:36
  218.6 13.1 %add_convert_fusion = bf16[2048,512]{1,0:T(8,128)(2,1)} fusion(bf16[2048,512]{1,0:T(8,128)(2,1)S(1)} %copy-done.5, bf16[512,512]{1,0:T(8,128)(2,1)S(1)} %copy-done.13, bf16[2048,6,512]{2,0,1:T(8,128)(2,1)} %copy_select_fusion, bf16[512,512]{1,0:T(8,128)(2,1)} %param.28), kind=kOutput, calls=%fused_computation.15 | convolution fusion | flops 2194669568 | bytes 19922944 | tf_op jit(solution)/shard_map/dot_general | solution.py:137
  (49 shorter events, 0.3 us)
Async XLA Ops:
  0.6 8.7 %copy-start = (bf16[512,512]{1,0:T(8,128)(2,1)S(1)}, bf16[512,512]{1,0:T(8,128)(2,1)}, u32[]{:S(2)}) copy-start(bf16[512,512]{1,0:T(8,128)(2,1)} %param.22) | copy-start | bytes 1572868
  2.4 88.3 %collective-permute-start.2 = (s32[128]{0:T(128)S(1)}, s32[128]{0:T(128)S(1)}, u32[]{:S(2)}, u32[]{:S(2)}) collective-permute-start(s32[128]{0:T(128)S(1)} %multiply_add_fusion.1), channel_id=1, source_target_pairs={{0,1},{1,2},{2,3},{3,4},{4,5},{5,6},{6,7},{7,8},{8,9},{9,10},{10,1... | collective-permute-start | bytes 1544 | tf_op jit(solution)/shard_map/ppermute | solution.py:19
  7.2 11.9 %copy-start.10 = (s32[2048,3]{0,1:T(4,128)S(1)}, s32[2048,3]{0,1:T(4,128)}, u32[]{:S(2)}) copy-start(s32[2048,3]{0,1:T(4,128)} %param.17) | copy-start | bytes 73732
  7.2 11.9 %copy-start.9 = (s32[2048,6]{0,1:T(8,128)S(1)}, s32[2048,6]{0,1:T(8,128)}, u32[]{:S(2)}) copy-start(s32[2048,6]{0,1:T(8,128)} %param.20) | copy-start | bytes 147460
  7.2 83.4 %collective-permute-start.3 = (s32[128]{0:T(128)S(1)}, s32[128]{0:T(128)S(1)}, u32[]{:S(2)}, u32[]{:S(2)}) collective-permute-start(s32[128]{0:T(128)S(1)} %multiply_add_fusion), channel_id=1, source_target_pairs={{1,0},{2,1},{3,2},{4,3},{5,4},{6,5},{7,6},{8,7},{9,8},{10,9},{11,1... | collective-permute-start | bytes 1544 | tf_op jit(solution)/shard_map/ppermute | solution.py:21
  12.2 1.3 copy-start.2
  13.5 8.0 %collective-permute-start = (bf16[128,512]{1,0:T(8,128)(2,1)S(1)}, bf16[128,512]{1,0:T(8,128)(2,1)S(1)}, u32[]{:S(2)}, u32[]{:S(2)}) collective-permute-start(bf16[128,512]{1,0:T(8,128)(2,1)S(1)} %get-tuple-element.14), channel_id=1, source_target_pairs={{0,1},{1,2},{2,3},{3,4},{4,5},{5,6},{6,7},{7,8},{8,9},{9,10},{10,1... | collective-permute-start | bytes 393224 | tf_op jit(solution)/shard_map/ppermute | solution.py:19
  17.2 6.3 %collective-permute-start.1 = (bf16[128,512]{1,0:T(8,128)(2,1)S(1)}, bf16[128,512]{1,0:T(8,128)(2,1)S(1)}, u32[]{:S(2)}, u32[]{:S(2)}) collective-permute-start(bf16[128,512]{1,0:T(8,128)(2,1)S(1)} %get-tuple-element.15), channel_id=1, source_target_pairs={{1,0},{2,1},{3,2},{4,3},{5,4},{6,5},{7,6},{8,7},{9,8},{10,9},{11,1... | collective-permute-start | bytes 393224 | tf_op jit(solution)/shard_map/ppermute | solution.py:21
  67.5 9.5 %copy-start.11 = (f32[83,2048]{1,0:T(8,128)S(1)}, f32[83,2048]{1,0:T(8,128)}, u32[]{:S(2)}) copy-start(f32[83,2048]{1,0:T(8,128)} %param.15) | copy-start | bytes 2039812
  67.5 9.5 %copy-start.14 = (bf16[512,83]{0,1:T(8,128)(2,1)S(1)}, bf16[512,83]{0,1:T(8,128)(2,1)}, u32[]{:S(2)}) copy-start(bf16[512,83]{0,1:T(8,128)(2,1)} %param.24) | copy-start | bytes 254980
  67.5 9.5 %copy-start.15 = (bf16[83,512]{1,0:T(8,128)(2,1)S(1)}, bf16[83,512]{1,0:T(8,128)(2,1)}, u32[]{:S(2)}) copy-start(bf16[83,512]{1,0:T(8,128)(2,1)} %param.23) | copy-start | bytes 254980
  77.1 7.2 %copy-start.16 = (bf16[83,512]{1,0:T(8,128)(2,1)S(1)}, bf16[83,512]{1,0:T(8,128)(2,1)}, u32[]{:S(2)}) copy-start(bf16[83,512]{1,0:T(8,128)(2,1)} %param.25) | copy-start | bytes 254980
  77.1 7.2 %copy-start.17 = (f32[83]{0:T(128)S(1)}, f32[83]{0:T(128)}, u32[]{:S(2)}) copy-start(f32[83]{0:T(128)} %param.21) | copy-start | bytes 1000
  84.1 1.6 copy-start.7
  85.7 5.0 %copy-start.6 = (bf16[2048,512]{1,0:T(8,128)(2,1)}, bf16[2048,512]{1,0:T(8,128)(2,1)S(1)}, u32[]{:S(2)}) copy-start(bf16[2048,512]{1,0:T(8,128)(2,1)S(1)} %multiply_convert_fusion) | copy-start | bytes 6291460
  86.1 20.3 %collective-permute-start.4 = (bf16[128,512]{1,0:T(8,128)(2,1)S(1)}, bf16[128,512]{1,0:T(8,128)(2,1)S(1)}, u32[]{:S(2)}, u32[]{:S(2)}) collective-permute-start(bf16[128,512]{1,0:T(8,128)(2,1)S(1)} %convolution_convert_fusion.3), channel_id=1, source_target_pairs={{0,1},{1,2},{2,3},{3,4},{4,5},{5,6},{6,7},{7,8},{8,9},{9,10},{10,1... | collective-permute-start | bytes 393224 | tf_op jit(solution)/shard_map/ppermute | solution.py:19
  88.0 18.4 %collective-permute-start.5 = (bf16[128,512]{1,0:T(8,128)(2,1)S(1)}, bf16[128,512]{1,0:T(8,128)(2,1)S(1)}, u32[]{:S(2)}, u32[]{:S(2)}) collective-permute-start(bf16[128,512]{1,0:T(8,128)(2,1)S(1)} %convolution_convert_fusion.2), channel_id=1, source_target_pairs={{1,0},{2,1},{3,2},{4,3},{5,4},{6,5},{7,6},{8,7},{9,8},{10,9},{11,1... | collective-permute-start | bytes 393224 | tf_op jit(solution)/shard_map/ppermute | solution.py:21
  90.7 20.0 %copy-start.3 = (bf16[2048,512]{1,0:T(8,128)(2,1)S(1)}, bf16[2048,512]{1,0:T(8,128)(2,1)}, u32[]{:S(2)}) copy-start(bf16[2048,512]{1,0:T(8,128)(2,1)} %param.16) | copy-start | bytes 6291460
  90.7 20.0 %copy-start.8 = (bf16[512,512]{1,0:T(8,128)(2,1)S(1)}, bf16[512,512]{1,0:T(8,128)(2,1)}, u32[]{:S(2)}) copy-start(bf16[512,512]{1,0:T(8,128)(2,1)} %param.26) | copy-start | bytes 1572868
  110.7 4.8 %copy-start.12 = (bf16[512,512]{1,0:T(8,128)(2,1)S(1)}, bf16[512,512]{1,0:T(8,128)(2,1)}, u32[]{:S(2)}) copy-start(bf16[512,512]{1,0:T(8,128)(2,1)} %param.27) | copy-start | bytes 1572868
  115.5 1.3 copy-start.4
  116.9 7.0 %collective-permute-start.6 = (bf16[128,512]{1,0:T(8,128)(2,1)S(1)}, bf16[128,512]{1,0:T(8,128)(2,1)S(1)}, u32[]{:S(2)}, u32[]{:S(2)}) collective-permute-start(bf16[128,512]{1,0:T(8,128)(2,1)S(1)} %get-tuple-element.12), channel_id=1, source_target_pairs={{0,1},{1,2},{2,3},{3,4},{4,5},{5,6},{6,7},{7,8},{8,9},{9,10},{10,1... | collective-permute-start | bytes 393224 | tf_op jit(solution)/shard_map/ppermute | solution.py:19
  121.7 6.3 %collective-permute-start.7 = (bf16[128,512]{1,0:T(8,128)(2,1)S(1)}, bf16[128,512]{1,0:T(8,128)(2,1)S(1)}, u32[]{:S(2)}, u32[]{:S(2)}) collective-permute-start(bf16[128,512]{1,0:T(8,128)(2,1)S(1)} %get-tuple-element.13), channel_id=1, source_target_pairs={{1,0},{2,1},{3,2},{4,3},{5,4},{6,5},{7,6},{8,7},{9,8},{10,9},{11,1... | collective-permute-start | bytes 393224 | tf_op jit(solution)/shard_map/ppermute | solution.py:21
  199.3 19.3 %copy-start.5 = (bf16[2048,512]{1,0:T(8,128)(2,1)S(1)}, bf16[2048,512]{1,0:T(8,128)(2,1)}, u32[]{:S(2)}) copy-start(bf16[2048,512]{1,0:T(8,128)(2,1)} %copy-done.4) | copy-start | bytes 6291460
  199.3 19.3 %copy-start.13 = (bf16[512,512]{1,0:T(8,128)(2,1)S(1)}, bf16[512,512]{1,0:T(8,128)(2,1)}, u32[]{:S(2)}) copy-start(bf16[512,512]{1,0:T(8,128)(2,1)} %param.29) | copy-start | bytes 1572868
  218.6 13.1 %copy-start.1 = (bf16[512,512]{1,0:T(8,128)(2,1)S(1)}, bf16[512,512]{1,0:T(8,128)(2,1)}, u32[]{:S(2)}) copy-start(bf16[512,512]{1,0:T(8,128)(2,1)} %param.22) | copy-start | bytes 1572868
where the time goes:
time: 234 us; the launch traced here: 232 us
  local copies, waits for them, and re-layouts  118 us (50%)
  other arithmetic  52.2 us (22%)
  matrix products  30.7 us (13%)
  starting transfers between devices  23.6 us (10%)
  waiting for transfers between devices  6.05 us (3%)
    gather x4, local copies, waits for them, and re-layouts, silu_sum(): jnp.take(source_table, positions.reshape(-1), axis=0)  113 us
    select_n x4, other arithmetic, silu_sum(): jnp.take(source_table, positions.reshape(-1), axis=0)  28.9 us
    scatter-add x2, other arithmetic, sum_into_nodes(): jax.ops.segment_sum(rows.astype(jnp.float32), node_ids, num_segments=node...  19.9 us
    ppermute x4, starting transfers between devices, extended(): lax.ppermute(tail, axis, [(i, (i + 1) % count) for i in range(ends)])  14.9 us
    dot_general x1, matrix products, shards(): jnp.dot(edges_sum, w_proc_out, preferred_element_type=jnp.float32)  13.1 us
    ppermute x4, starting transfers between devices, extended(): lax.ppermute(head, axis, [((i + 1) % count, i) for i in range(ends)])  8.7 us
    dot_general x1, matrix products, shards(): lax.dot_general(w_dec_out, decoded, (((0,), (1,)), ((), ())), preferred_e...  7.01 us
    ppermute x4, waiting for transfers between devices, extended(): lax.ppermute(head, axis, [((i + 1) % count, i) for i in range(ends)])  6.04 us
  transfers between devices with their start and end apart: 8, of which 2 were waited for; matrix products, arithmetic and copies ran while one was open for 36% of the time, Pallas kernels for 0%

commit v1 on v0

v1 whole, which is shorter than its diff:
```python
import functools

import jax
import jax.numpy as jnp
from jax import lax
from jax.experimental import pallas as pl
from jax.experimental.pallas import tpu as pltpu
from jax.sharding import PartitionSpec as P

HALO = 128
KD = 3
KN = 6
BLOCK = 256
UNROLL = 8
PAD = 8


def dot(left, right, left_dim=1, right_dim=0):
    return lax.dot_general(
        left, right, (((left_dim,), (right_dim,)), ((), ())), preferred_element_type=jnp.float32
    )


def half_silu(half):
    return half * jnp.tanh(half) + half


def put_rows(table, first, values):
    count = values.shape[0]
    for part in range(values.shape[1] // 128):
        table[pl.ds(first + part, count, stride=4), :] = values[:, part * 128 : part * 128 + 128]


def get_rows(table, first, count):
    return jnp.concatenate(
        [table[pl.ds(first + part, count, stride=4), :] for part in range(4)], axis=1
    )


def gather_sum(table, index, rows, fanout, base, total, first):
    upper = lax.broadcasted_iota(jnp.int32, (8, 128), 0) >= 4

    def body(step, carry):
        for inner in range(UNROLL):
            pair = step * UNROLL + inner
            point = first + 2 * pair
            spot = pl.ds(pl.multiple_of(pair * 8, 8), 8)
            own = base[spot, :]
            summed = None
            for edge in range(fanout):
                left = table[pl.ds(index[edge * rows + point], 8), :]
                right = table[pl.ds(index[edge * rows + point + 1], 8), :]
                term = half_silu(jnp.where(upper, right, left) + own)
                summed = term if summed is None else summed + term
            total[spot, :] = summed
        return carry

    lax.fori_loop(0, BLOCK // 2 // UNROLL, body, 0)


def one_hot(ids, first):
    rows = lax.broadcasted_iota(jnp.int32, (BLOCK, ids.shape[1]), 0) + first
    return jnp.where(rows == ids, 1.0, 0.0).astype(jnp.bfloat16)


def kernel(
    bands,
    m2g_index,
    mesh_index,
    state,
    latent,
    local_ids,
    lower_ids,
    upper_ids,
    gain,
    w_dec_mesh,
    w_dec_grid,
    w_dec_out,
    w_enc,
    w_enc_out,
    w_proc_src,
    w_proc_dst,
    w_proc_out,
    new_state,
    mesh_out,
    table,
    base,
    total,
    message,
    collected,
    middle,
    halo_out,
    halo_in,
    halo_in2,
    rim,
    rim_ids,
    send_sem,
    recv_sem,
):
    me = lax.axis_index("band")
    rows = latent.shape[0]
    points = state.shape[1]
    blocks = rows // BLOCK
    has = (me > 0, me < bands - 1)
    other = (me - 1, me + 1)

    def copy(number, side, source, target):
        return pltpu.make_async_remote_copy(
            src_ref=source,
            dst_ref=target,
            send_sem=send_sem.at[2 * number + side],
            recv_sem=recv_sem.at[2 * number + side],
            device_id={"band": other[side]},
            device_id_type=pl.DeviceIdType.MESH,
        )

    def halo_copy(number, side, landing):
        return copy(number, side, halo_out.at[number // 3, side], landing.at[1 - side])

    def ids_copy(side):
        return copy(1, side, (lower_ids, upper_ids)[side], rim_ids.at[1 - side])

    def rim_copy(side):
        start = 0 if side == 0 else points - BLOCK
        return copy(
            2, side, message.at[pl.ds(start, BLOCK)], rim.at[pl.ds((1 - side) * BLOCK, BLOCK)]
        )

    def start(make):
        for side in (0, 1):

            @pl.when(has[side])
            def _():
                make(side).start()

    def finish(make):
        for side in (0, 1):

            @pl.when(has[side])
            def _():
                make(side).wait_send()

            @pl.when(has[1 - side])
            def _():
                make(side).wait_recv()

    proj_copy = functools.partial(halo_copy, 0, landing=halo_in)
    send_copy = functools.partial(halo_copy, 3, landing=halo_in2)

    def block_of(step):
        return jnp.where(step == 0, 0, jnp.where(step == 1, blocks - 1, step - 1))

    def unpack(landing):
        for side in (0, 1):
            first = PAD + side * 4 * (HALO + rows)

            @pl.when(has[side])
            def _():
                put_rows(table, first, 0.5 * landing[side].astype(jnp.float32))

    def fill_block(step, source, weight, number):
        block = block_of(step)
        row = pl.multiple_of(block * BLOCK, BLOCK)
        values = dot(source[pl.ds(row, BLOCK), :], weight[...])
        put_rows(table, PAD + 4 * (HALO + row), 0.5 * values)
        return values

    barrier = pltpu.get_barrier_semaphore()
    for side in (0, 1):

        @pl.when(has[side])
        def _():
            pl.semaphore_signal(
                barrier,
                inc=1,
                device_id={"band": other[side]},
                device_id_type=pl.DeviceIdType.MESH,
            )

    pl.semaphore_wait(barrier, jnp.where(me > 0, 1, 0) + jnp.where(me < bands - 1, 1, 0))

    for side in (0, 1):

        @pl.when(jnp.logical_not(has[side]))
        def _():
            first = PAD + side * 4 * (HALO + rows)
            table[pl.ds(first, 4 * HALO), :] = jnp.zeros((4 * HALO, 128), jnp.float32)
            rim[pl.ds(side * BLOCK, BLOCK), :] = jnp.zeros((BLOCK, rim.shape[1]), rim.dtype)
            rim_ids[side] = jnp.full((1, BLOCK), -1, jnp.int32)

    start(ids_copy)

    def project(step, carry):
        values = fill_block(step, latent, w_dec_mesh, 0)

        @pl.when(step == 0)
        def _():
            halo_out[0, 0] = values[:HALO].astype(jnp.bfloat16)

        @pl.when(step == 1)
        def _():
            halo_out[0, 1] = values[BLOCK - HALO :].astype(jnp.bfloat16)
            start(proj_copy)

        return carry

    lax.fori_loop(0, blocks, project, 0)
    finish(proj_copy)
    unpack(halo_in)

    def decode(step, carry):
        block = block_of(step)
        point = pl.multiple_of(block * BLOCK, BLOCK)
        columns = pl.ds(point, BLOCK)
        cells = state[:, columns]
        put_rows(base, 0, 0.5 * dot(cells.astype(jnp.bfloat16), w_dec_grid[...], 0, 0))
        gather_sum(table, m2g_index, points, KD, base, total, point)
        decoded = get_rows(total, 0, BLOCK).astype(jnp.bfloat16)
        fresh = cells + dot(w_dec_out[...], decoded, 1, 1)
        new_state[:, columns] = fresh
        average = jnp.mean(fresh, axis=0, keepdims=True)
        centered = fresh - average
        variance = jnp.mean(centered * centered, axis=0, keepdims=True)
        normed = (centered * lax.rsqrt(variance + 1e-05) * gain[...]).astype(jnp.bfloat16)
        sent = half_silu(0.5 * dot(normed, w_enc[...], 0, 0))
        message[columns, :] = sent.astype(jnp.bfloat16)

        @pl.when(step == 1)
        def _():
            start(rim_copy)

        return carry

    lax.fori_loop(0, points // BLOCK, decode, 0)

    def collect(block, carry):
        row = pl.multiple_of(block * BLOCK, BLOCK)
        collected[pl.ds(row, BLOCK), :] = dot(one_hot(local_ids[...], row), message[...])
        return carry

    lax.fori_loop(0, blocks, collect, 0)
    finish(ids_copy)
    finish(rim_copy)

    def update(step, carry):
        block = block_of(step)
        row = pl.multiple_of(block * BLOCK, BLOCK)
        span = pl.ds(row, BLOCK)
        encoded = collected[span, :]
        for side in (0, 1):
            encoded += dot(one_hot(rim_ids[side], row), rim[pl.ds(side * BLOCK, BLOCK), :])
        mixed = latent[span, :].astype(jnp.float32) + dot(
            encoded.astype(jnp.bfloat16), w_enc_out[...]
        )
        middle[span, :] = mixed.astype(jnp.bfloat16)
        values = fill_block(step, middle, w_proc_src, 1)

        @pl.when(step == 0)
        def _():
            halo_out[1, 0] = values[:HALO].astype(jnp.bfloat16)

        @pl.when(step == 1)
        def _():
            halo_out[1, 1] = values[BLOCK - HALO :].astype(jnp.bfloat16)
            start(send_copy)

        return carry

    lax.fori_loop(0, blocks, update, 0)
    finish(send_copy)
    unpack(halo_in2)

    def process(block, carry):
        row = pl.multiple_of(block * BLOCK, BLOCK)
        span = pl.ds(row, BLOCK)
        kept = middle[span, :]
        put_rows(base, 0, 0.5 * dot(kept, w_proc_dst[...]))
        gather_sum(table, mesh_index, rows, KN, base, total, row)
        edges = get_rows(total, 0, BLOCK).astype(jnp.bfloat16)
        result = kept.astype(jnp.float32) + dot(edges, w_proc_out[...])
        mesh_out[span, :] = result.astype(jnp.bfloat16)
        return carry

    lax.fori_loop(0, blocks, process, 0)


def shards(
    bands,
    state,
    mesh_latent,
    m2g_src,
    g2m_owner,
    g2m_node,
    mesh_src,
    norm_gain,
    w_dec_mesh,
    w_dec_grid,
    w_dec_out,
    w_enc,
    w_enc_out,
    w_proc_src,
    w_proc_dst,
    w_proc_out,
):
    position = lax.axis_index("band")
    rows, width = mesh_latent.shape
    points = state.shape[1]

    def places(sources):
        count = sources.shape[0]
        parity = lax.broadcasted_iota(jnp.int32, (1, count), 1) % 2
        local = sources.T - (position * rows - HALO)
        return (4 * local + (PAD - 4 * parity)).reshape(-1)

    relative = g2m_owner.T - position
    nodes = g2m_node.T
    local_ids = jnp.where(relative == 0, nodes, -1)
    lower_ids = jnp.where(relative[:, :BLOCK] == -1, nodes[:, :BLOCK], -1)
    upper_ids = jnp.where(relative[:, points - BLOCK :] == 1, nodes[:, points - BLOCK :], -1)
    vmem = pl.BlockSpec(memory_space=pltpu.VMEM)
    smem = pl.BlockSpec(memory_space=pltpu.SMEM)
    return pl.pallas_call(
        functools.partial(kernel, bands),
        out_shape=(
            jax.ShapeDtypeStruct(state.shape, jnp.float32),
            jax.ShapeDtypeStruct(mesh_latent.shape, jnp.bfloat16),
        ),
        in_specs=[smem, smem] + [vmem] * 14,
        out_specs=(vmem, vmem),
        scratch_shapes=[
            pltpu.VMEM((PAD + 4 * (rows + 2 * HALO) + 8, 128), jnp.float32),
            pltpu.VMEM((4 * BLOCK, 128), jnp.float32),
            pltpu.VMEM((4 * BLOCK, 128), jnp.float32),
            pltpu.VMEM((points, width), jnp.bfloat16),
            pltpu.VMEM((rows, width), jnp.float32),
            pltpu.VMEM((rows, width), jnp.bfloat16),
            pltpu.VMEM((2, 2, HALO, width), jnp.bfloat16),
            pltpu.VMEM((2, HALO, width), jnp.bfloat16),
            pltpu.VMEM((2, HALO, width), jnp.bfloat16),
            pltpu.VMEM((2 * BLOCK, width), jnp.bfloat16),
            pltpu.VMEM((2, 1, BLOCK), jnp.int32),
            pltpu.SemaphoreType.DMA((8,)),
            pltpu.SemaphoreType.DMA((8,)),
        ],
        compiler_params=pltpu.CompilerParams(
            collective_id=0, has_side_effects=True, vmem_limit_bytes=48 * 1024 * 1024
        ),
        name="handover",
    )(
        places(m2g_src),
        places(mesh_src),
        state,
        mesh_latent,
        local_ids,
        lower_ids,
        upper_ids,
        norm_gain[:, None],
        w_dec_mesh,
        w_dec_grid,
        w_dec_out.T,
        w_enc,
        w_enc_out,
        w_proc_src,
        w_proc_dst,
        w_proc_out,
    )


def solution(mesh):
    placed = (
        P(None, ("groups", "band")),
        P(("groups", "band"), None),
        P(("groups", "band"), None),
        P(("groups", "band"), None),
        P(("groups", "band"), None),
        P(("groups", "band"), None),
        P(),
        P(),
        P(),
        P(),
        P(),
        P(),
        P(),
        P(),
        P(),
    )
    return jax.shard_map(
        functools.partial(shards, mesh.shape["band"]),
        mesh=mesh,
        in_specs=placed,
        out_specs=(P(None, ("groups", "band")), P(("groups", "band"), None)),
        check_vma=False,
    )
```

time: 234 us -> 71.1 us (0.30)
  local copies, waits for them, and re-layouts: 118 us -> 13.7 us
  Pallas kernels: 0 us -> 53 us
  other arithmetic: 52.2 us -> 3.06 us
  matrix products: 30.7 us -> 0 us
  starting transfers between devices: 23.6 us -> 0 us
  waiting for transfers between devices: 6.05 us -> 0 us
    gather x4 -> x0, local copies, waits for them, and re-layouts: 113 us -> none  [silu_sum(): jnp.take(source_table, positions.reshape(-1), axis=0)]
    pallas_call x0 -> x1, Pallas kernels: none -> 53 us  [shards(): pl.pallas_call(functools.partial(kernel, bands), out_shape=(jax.ShapeDtyp...]
    dot_general x8 -> x0, matrix products: 30.7 us -> none  [the longest x1 13.1 us: shards(): jnp.dot(edges_sum, w_proc_out, preferred_element_type=jnp.float32)]
    select_n x5 -> x2, other arithmetic: 29.6 us -> 1.44 us  [the longest x1 0.73 us: shards(): local_ids = jnp.where(relative == 0, nodes, -1)]
    ppermute x8 -> x0, starting transfers between devices: 23.6 us -> none  [the longest x4 14.9 us: extended(): lax.ppermute(tail, axis, [(i, (i + 1) % count) for i in range(ends)])]
    scatter-add x2 -> x0, other arithmetic: 19.9 us -> none  [sum_into_nodes(): jax.ops.segment_sum(rows.astype(jnp.float32), node_ids, num_segments=node...]
    unnamed x36 -> x20, local copies, waits for them, and re-layouts: 1.46 us -> 12.9 us
    ppermute x8 -> x0, waiting for transfers between devices: 6.05 us -> none  [the longest x4 6.04 us: extended(): lax.ppermute(head, axis, [((i + 1) % count, i) for i in range(ends)])]
  transfers between devices with their start and end apart: 8 -> 0, of which waited for: 2 -> 0; matrix products, arithmetic and copies ran while one was open for 36% -> 0% of each run, Pallas kernels for 0% -> 0%
where the time goes in v1:
time: 71.1 us; the launch traced here: 70.4 us
  Pallas kernels  53 us (75%)
  local copies, waits for them, and re-layouts  13.7 us (19%)
  other arithmetic  3.06 us (4%)
    pallas_call x1, Pallas kernels, shards(): pl.pallas_call(functools.partial(kernel, bands), out_shape=(jax.ShapeDtyp...  53 us
    unnamed x20, local copies, waits for them, and re-layouts  12.9 us
    add x2, other arithmetic, places(): return (4 * local + (PAD - 4 * parity)).reshape(-1)  1.62 us

profile of v1, /device:TPU:1, one launch (start us, length us, event | category | flops | bytes accessed | tf_op | source)
XLA Modules:
  0.0 70.4 jit_solution(15165050634256159004)
XLA Ops:
  0.6 0.7 %compare_select_fusion = (s32[1,2048]{1,0:T(1,128)S(1)}, s32[1,2048]{1,0:T(1,128)S(1)}) fusion(s32[2048,1]{0,1:T(1,128)} %param.19, s32[2048,1]{0,1:T(1,128)} %param.18, s32[]{:T(128)S(6)} %axis_index.12), kind=kLoop, calls=%fused_computation.2 | loop fusion | flops 6144 | bytes 32772 | tf_op jit(solution)/shard_map/jit(_where)/select_n | solution.py:317
  1.4 0.7 compare_select_fusion.1
  2.1 0.8 %add_bitcast_fusion.1 = s32[3,2048]{1,0:T(4,128)S(1)} fusion(s32[2048,3]{0,1:T(4,128)} %param.17, s32[2048]{0:T(1024)S(1)} %fusion.1, s32[]{:T(128)S(6)} %sub.50), kind=kLoop, calls=%fused_computation.1 | loop fusion | flops 18432 | bytes 57348 | tf_op jit(solution)/shard_map/add | solution.py:313
  2.9 0.8 %copy.17.gain = f32[83,1]{1,0:T(8,128)S(1)} copy(f32[83,1]{0,1:T(1,128)} %bitcast.13) | data formatting | bytes 664 | tf_op jit(solution)/shard_map/broadcast_in_dim | solution.py:357
  3.7 0.9 %add_bitcast_fusion = s32[6,2048]{1,0:T(8,128)S(1)} fusion(s32[2048,6]{0,1:T(8,128)} %param.20, s32[2048]{0:T(1024)S(1)} %fusion.1, s32[]{:T(128)S(6)} %sub.50), kind=kLoop, calls=%fused_computation | loop fusion | flops 36864 | bytes 106500 | tf_op jit(solution)/shard_map/add | solution.py:313
  4.5 0.0 copy-start
  4.5 1.1 %copy-done = f32[83,2048]{1,0:T(8,128)S(1)} copy-done((f32[83,2048]{1,0:T(8,128)S(1)}, f32[83,2048]{1,0:T(8,128)}, u32[]{:S(2)}) %copy-start) | copy-done | bytes 679960
  5.6 0.0 copy-start.1
  5.6 1.0 %copy-done.1 = bf16[512,512]{1,0:T(8,128)(2,1)S(1)} copy-done((bf16[512,512]{1,0:T(8,128)(2,1)S(1)}, bf16[512,512]{1,0:T(8,128)(2,1)}, u32[]{:S(2)}) %copy-start.1) | copy-done | bytes 524312
  6.7 0.0 copy-start.2
  6.7 1.0 %copy-done.2 = bf16[512,512]{1,0:T(8,128)(2,1)S(1)} copy-done((bf16[512,512]{1,0:T(8,128)(2,1)S(1)}, bf16[512,512]{1,0:T(8,128)(2,1)}, u32[]{:S(2)}) %copy-start.2) | copy-done | bytes 524312
  7.7 0.0 copy-start.3
  7.7 1.0 %copy-done.3 = bf16[512,512]{1,0:T(8,128)(2,1)S(1)} copy-done((bf16[512,512]{1,0:T(8,128)(2,1)S(1)}, bf16[512,512]{1,0:T(8,128)(2,1)}, u32[]{:S(2)}) %copy-start.3) | copy-done | bytes 524312
  8.8 0.0 copy-start.4
  8.8 1.0 %copy-done.4 = bf16[512,512]{1,0:T(8,128)(2,1)S(1)} copy-done((bf16[512,512]{1,0:T(8,128)(2,1)S(1)}, bf16[512,512]{1,0:T(8,128)(2,1)}, u32[]{:S(2)}) %copy-start.4) | copy-done | bytes 524312
  9.8 0.0 copy-start.5
  9.8 1.0 %copy-done.5 = bf16[512,512]{1,0:T(8,128)(2,1)S(1)} copy-done((bf16[512,512]{1,0:T(8,128)(2,1)S(1)}, bf16[512,512]{1,0:T(8,128)(2,1)}, u32[]{:S(2)}) %copy-start.5) | copy-done | bytes 524312
  10.9 0.0 copy-start.6
  10.9 0.9 %copy-done.6 = bf16[83,512]{1,0:T(8,128)(2,1)S(1)} copy-done((bf16[83,512]{1,0:T(8,128)(2,1)S(1)}, bf16[83,512]{1,0:T(8,128)(2,1)}, u32[]{:S(2)}) %copy-start.6) | copy-done | bytes 85016
  11.7 0.0 copy-start.7
  11.7 0.9 %copy-done.7 = bf16[512,83]{0,1:T(8,128)(2,1)S(1)} copy-done((bf16[512,83]{0,1:T(8,128)(2,1)S(1)}, bf16[512,83]{0,1:T(8,128)(2,1)}, u32[]{:S(2)}) %copy-start.7) | copy-done | bytes 85016
  12.6 0.0 copy-start.8
  12.6 0.9 %copy-done.8 = bf16[83,512]{1,0:T(8,128)(2,1)S(1)} copy-done((bf16[83,512]{1,0:T(8,128)(2,1)S(1)}, bf16[83,512]{1,0:T(8,128)(2,1)}, u32[]{:S(2)}) %copy-start.8) | copy-done | bytes 85016
  13.5 53.0 %handover.1 = (f32[83,2048]{1,0:T(8,128)S(1)}, bf16[2048,512]{1,0:T(8,128)(2,1)}) custom-call(s32[6144]{0:T(1024)S(1)} %reshape.63.m2g_index, s32[12288]{0:T(1024)S(1)} %reshape.64.mesh_index, f32[83,2048]{1,0:T(8,128)S(1)} %copy-done, bf16[2048,512]{1,0:T(8,128)(2,1)} %latent.1, s32[1,2048]{1,0:T(1,128)S(1)} %get-tuple-element.2.local_ids, ...), custom_call_target="tpu_custom_call" | custom-call | tf_op jit(solution)/shard_map/handover/pallas_call | solution.py:322
  66.5 0.9 %copy.20 = f32[83,2048]{1,0:T(8,128)} copy(f32[83,2048]{1,0:T(8,128)S(1)} %get-tuple-element.8) | data formatting | bytes 1359872
  67.4 3.0 %copy.21 = bf16[2048,512]{1,0:T(8,128)(2,1)} copy(bf16[2048,512]{1,0:T(8,128)(2,1)} %get-tuple-element.9) | data formatting | bytes 4194304
  (3 shorter events, 0.0 us)
Async XLA Ops:
  4.5 1.1 %copy-start = (f32[83,2048]{1,0:T(8,128)S(1)}, f32[83,2048]{1,0:T(8,128)}, u32[]{:S(2)}) copy-start(f32[83,2048]{1,0:T(8,128)} %state.1) | copy-start | bytes 2039812
  5.6 1.0 %copy-start.1 = (bf16[512,512]{1,0:T(8,128)(2,1)S(1)}, bf16[512,512]{1,0:T(8,128)(2,1)}, u32[]{:S(2)}) copy-start(bf16[512,512]{1,0:T(8,128)(2,1)} %w_dec_mesh.1) | copy-start | bytes 1572868
  6.7 1.0 %copy-start.2 = (bf16[512,512]{1,0:T(8,128)(2,1)S(1)}, bf16[512,512]{1,0:T(8,128)(2,1)}, u32[]{:S(2)}) copy-start(bf16[512,512]{1,0:T(8,128)(2,1)} %w_enc_out.1) | copy-start | bytes 1572868
  7.7 1.0 %copy-start.3 = (bf16[512,512]{1,0:T(8,128)(2,1)S(1)}, bf16[512,512]{1,0:T(8,128)(2,1)}, u32[]{:S(2)}) copy-start(bf16[512,512]{1,0:T(8,128)(2,1)} %w_proc_src.1) | copy-start | bytes 1572868
  8.8 1.0 %copy-start.4 = (bf16[512,512]{1,0:T(8,128)(2,1)S(1)}, bf16[512,512]{1,0:T(8,128)(2,1)}, u32[]{:S(2)}) copy-start(bf16[512,512]{1,0:T(8,128)(2,1)} %w_proc_dst.1) | copy-start | bytes 1572868
  9.8 1.0 %copy-start.5 = (bf16[512,512]{1,0:T(8,128)(2,1)S(1)}, bf16[512,512]{1,0:T(8,128)(2,1)}, u32[]{:S(2)}) copy-start(bf16[512,512]{1,0:T(8,128)(2,1)} %w_proc_out.1) | copy-start | bytes 1572868
  10.9 0.9 %copy-start.6 = (bf16[83,512]{1,0:T(8,128)(2,1)S(1)}, bf16[83,512]{1,0:T(8,128)(2,1)}, u32[]{:S(2)}) copy-start(bf16[83,512]{1,0:T(8,128)(2,1)} %w_dec_grid.1) | copy-start | bytes 254980
  11.7 0.9 %copy-start.7 = (bf16[512,83]{0,1:T(8,128)(2,1)S(1)}, bf16[512,83]{0,1:T(8,128)(2,1)}, u32[]{:S(2)}) copy-start(bf16[512,83]{0,1:T(8,128)(2,1)} %param.24) | copy-start | bytes 254980
  12.6 0.9 %copy-start.8 = (bf16[83,512]{1,0:T(8,128)(2,1)S(1)}, bf16[83,512]{1,0:T(8,128)(2,1)}, u32[]{:S(2)}) copy-start(bf16[83,512]{1,0:T(8,128)(2,1)} %w_enc.1) | copy-start | bytes 254980

commit v2 on v1

--- a/solution.py
+++ b/solution.py
@@ -11,7 +11,7 @@
 KD = 3
 KN = 6
 BLOCK = 256
-UNROLL = 8
+UNROLL = 16
 PAD = 8
 
 
@@ -41,18 +41,22 @@
     upper = lax.broadcasted_iota(jnp.int32, (8, 128), 0) >= 4
 
     def body(step, carry):
+        point = pl.multiple_of(first + 2 * UNROLL * step, 2 * UNROLL)
+        views = [
+            index.at[pl.ds(edge * rows + point, 2 * UNROLL)] for edge in range(fanout)
+        ]
+        near = base.at[pl.ds(pl.multiple_of(4 * point, 8 * UNROLL), 8 * UNROLL)]
+        far = total.at[pl.ds(pl.multiple_of(step * 8 * UNROLL, 8 * UNROLL), 8 * UNROLL)]
         for inner in range(UNROLL):
-            pair = step * UNROLL + inner
-            point = first + 2 * pair
-            spot = pl.ds(pl.multiple_of(pair * 8, 8), 8)
-            own = base[spot, :]
+            spot = pl.ds(8 * inner, 8)
+            own = near[spot, :]
             summed = None
             for edge in range(fanout):
-                left = table[pl.ds(index[edge * rows + point], 8), :]
-                right = table[pl.ds(index[edge * rows + point + 1], 8), :]
+                left = table[pl.ds(views[edge][2 * inner], 8), :]
+                right = table[pl.ds(views[edge][2 * inner + 1], 8), :]
                 term = half_silu(jnp.where(upper, right, left) + own)
                 summed = term if summed is None else summed + term
-            total[spot, :] = summed
+            far[spot, :] = summed
         return carry
 
     lax.fori_loop(0, BLOCK // 2 // UNROLL, body, 0)
@@ -67,20 +71,19 @@
     bands,
     m2g_index,
     mesh_index,
-    state,
-    latent,
-    local_ids,
-    lower_ids,
-    upper_ids,
-    gain,
-    w_dec_mesh,
-    w_dec_grid,
-    w_dec_out,
-    w_enc,
-    w_enc_out,
-    w_proc_src,
-    w_proc_dst,
-    w_proc_out,
+    owner,
+    node,
+    gain_row,
+    far_state,
+    far_latent,
+    far_w_dec_mesh,
+    far_w_dec_grid,
+    far_w_dec_out,
+    far_w_enc,
+    far_w_enc_out,
+    far_w_proc_src,
+    far_w_proc_dst,
+    far_w_proc_out,
     new_state,
     mesh_out,
     table,
@@ -96,6 +99,20 @@
     rim_ids,
     send_sem,
     recv_sem,
+    load_sem,
+    window_ids,
+    local_ids,
+    gain,
+    state,
+    latent,
+    w_dec_mesh,
+    w_dec_grid,
+    w_dec_out,
+    w_enc,
+    w_enc_out,
+    w_proc_src,
+    w_proc_dst,
+    w_proc_out,
 ):
     me = lax.axis_index("band")
     rows = latent.shape[0]
@@ -118,7 +135,7 @@
         return copy(number, side, halo_out.at[number // 3, side], landing.at[1 - side])
 
     def ids_copy(side):
-        return copy(1, side, (lower_ids, upper_ids)[side], rim_ids.at[1 - side])
+        return copy(1, side, window_ids.at[side], rim_ids.at[1 - side])
 
     def rim_copy(side):
         start = 0 if side == 0 else points - BLOCK
@@ -165,6 +182,32 @@
         put_rows(table, PAD + 4 * (HALO + row), 0.5 * values)
         return values
 
+    middle_rows = rows - 2 * BLOCK
+
+    def latent_part(first, count):
+        return far_latent.at[pl.ds(first, count)], latent.at[pl.ds(first, count)]
+
+    loads = dict(
+        latent_first=latent_part(0, BLOCK),
+        w_dec_mesh=(far_w_dec_mesh, w_dec_mesh),
+        latent_last=latent_part(rows - BLOCK, BLOCK),
+        latent_middle=latent_part(BLOCK, middle_rows),
+        w_dec_grid=(far_w_dec_grid, w_dec_grid),
+        state=(far_state, state),
+        w_dec_out=(far_w_dec_out, w_dec_out),
+        w_enc=(far_w_enc, w_enc),
+        w_enc_out=(far_w_enc_out, w_enc_out),
+        w_proc_src=(far_w_proc_src, w_proc_src),
+        w_proc_dst=(far_w_proc_dst, w_proc_dst),
+        w_proc_out=(far_w_proc_out, w_proc_out),
+    )
+    loads = {
+        name: pltpu.make_async_copy(source, target, load_sem.at[number])
+        for number, (name, (source, target)) in enumerate(loads.items())
+    }
+    for load in loads.values():
+        load.start()
+
     barrier = pltpu.get_barrier_semaphore()
     for side in (0, 1):
 
@@ -188,7 +231,17 @@
             rim[pl.ds(side * BLOCK, BLOCK), :] = jnp.zeros((BLOCK, rim.shape[1]), rim.dtype)
             rim_ids[side] = jnp.full((1, BLOCK), -1, jnp.int32)
 
+    relative = owner[...] - me
+    local_ids[...] = jnp.where(relative == 0, node[...], -1)
+    window_ids[0] = jnp.where(relative == -1, node[...], -1)[:, :BLOCK]
+    window_ids[1] = jnp.where(relative == 1, node[...], -1)[:, points - BLOCK :]
     start(ids_copy)
+    channels = gain_row.shape[1]
+    square = (channels, channels)
+    same = lax.broadcasted_iota(jnp.int32, square, 0) == lax.broadcasted_iota(jnp.int32, square, 1)
+    gain[...] = jnp.sum(jnp.where(same, gain_row[...], 0.0), axis=1, keepdims=True)
+    for name in ("latent_first", "w_dec_mesh", "latent_last"):
+        loads[name].wait()
 
     def project(step, carry):
         values = fill_block(step, latent, w_dec_mesh, 0)
@@ -201,10 +254,23 @@
         def _():
             halo_out[0, 1] = values[BLOCK - HALO :].astype(jnp.bfloat16)
             start(proj_copy)
+            loads["latent_middle"].wait()
 
         return carry
 
     lax.fori_loop(0, blocks, project, 0)
+    for name in ("w_dec_grid", "state"):
+        loads[name].wait()
+
+    def receive(block, carry):
+        point = pl.multiple_of(block * BLOCK, BLOCK)
+        cells = state[:, pl.ds(point, BLOCK)].astype(jnp.bfloat16)
+        put_rows(base, 4 * point, 0.5 * dot(cells, w_dec_grid[...], 0, 0))
+        return carry
+
+    lax.fori_loop(0, points // BLOCK, receive, 0)
+    for name in ("w_dec_out", "w_enc"):
+        loads[name].wait()
     finish(proj_copy)
     unpack(halo_in)
 
@@ -213,7 +279,6 @@
         point = pl.multiple_of(block * BLOCK, BLOCK)
         columns = pl.ds(point, BLOCK)
         cells = state[:, columns]
-        put_rows(base, 0, 0.5 * dot(cells.astype(jnp.bfloat16), w_dec_grid[...], 0, 0))
         gather_sum(table, m2g_index, points, KD, base, total, point)
         decoded = get_rows(total, 0, BLOCK).astype(jnp.bfloat16)
         fresh = cells + dot(w_dec_out[...], decoded, 1, 1)
@@ -239,6 +304,8 @@
         return carry
 
     lax.fori_loop(0, blocks, collect, 0)
+    for name in ("w_enc_out", "w_proc_src", "w_proc_dst", "w_proc_out"):
+        loads[name].wait()
     finish(ids_copy)
     finish(rim_copy)
 
@@ -264,6 +331,7 @@
             halo_out[1, 1] = values[BLOCK - HALO :].astype(jnp.bfloat16)
             start(send_copy)
 
+        put_rows(base, 4 * row, 0.5 * dot(middle[span, :], w_proc_dst[...]))
         return carry
 
     lax.fori_loop(0, blocks, update, 0)
@@ -273,11 +341,9 @@
     def process(block, carry):
         row = pl.multiple_of(block * BLOCK, BLOCK)
         span = pl.ds(row, BLOCK)
-        kept = middle[span, :]
-        put_rows(base, 0, 0.5 * dot(kept, w_proc_dst[...]))
         gather_sum(table, mesh_index, rows, KN, base, total, row)
         edges = get_rows(total, 0, BLOCK).astype(jnp.bfloat16)
-        result = kept.astype(jnp.float32) + dot(edges, w_proc_out[...])
+        result = middle[span, :].astype(jnp.float32) + dot(edges, w_proc_out[...])
         mesh_out[span, :] = result.astype(jnp.bfloat16)
         return carry
 
@@ -312,24 +378,32 @@
         local = sources.T - (position * rows - HALO)
         return (4 * local + (PAD - 4 * parity)).reshape(-1)
 
-    relative = g2m_owner.T - position
-    nodes = g2m_node.T
-    local_ids = jnp.where(relative == 0, nodes, -1)
-    lower_ids = jnp.where(relative[:, :BLOCK] == -1, nodes[:, :BLOCK], -1)
-    upper_ids = jnp.where(relative[:, points - BLOCK :] == 1, nodes[:, points - BLOCK :], -1)
     vmem = pl.BlockSpec(memory_space=pltpu.VMEM)
     smem = pl.BlockSpec(memory_space=pltpu.SMEM)
+    hbm = pl.BlockSpec(memory_space=pltpu.HBM)
+    near = (
+        state,
+        mesh_latent,
+        w_dec_mesh,
+        w_dec_grid,
+        w_dec_out.T,
+        w_enc,
+        w_enc_out,
+        w_proc_src,
+        w_proc_dst,
+        w_proc_out,
+    )
     return pl.pallas_call(
         functools.partial(kernel, bands),
         out_shape=(
             jax.ShapeDtypeStruct(state.shape, jnp.float32),
             jax.ShapeDtypeStruct(mesh_latent.shape, jnp.bfloat16),
         ),
-        in_specs=[smem, smem] + [vmem] * 14,
+        in_specs=[smem] * 2 + [vmem] * 3 + [hbm] * 10,
         out_specs=(vmem, vmem),
         scratch_shapes=[
             pltpu.VMEM((PAD + 4 * (rows + 2 * HALO) + 8, 128), jnp.float32),
-            pltpu.VMEM((4 * BLOCK, 128), jnp.float32),
+            pltpu.VMEM((4 * points, 128), jnp.float32),
             pltpu.VMEM((4 * BLOCK, 128), jnp.float32),
             pltpu.VMEM((points, width), jnp.bfloat16),
             pltpu.VMEM((rows, width), jnp.float32),
@@ -341,28 +415,23 @@
             pltpu.VMEM((2, 1, BLOCK), jnp.int32),
             pltpu.SemaphoreType.DMA((8,)),
             pltpu.SemaphoreType.DMA((8,)),
+            pltpu.SemaphoreType.DMA((12,)),
+            pltpu.VMEM((2, 1, BLOCK), jnp.int32),
+            pltpu.VMEM((1, points), jnp.int32),
+            pltpu.VMEM((state.shape[0], 1), jnp.float32),
+            *[pltpu.VMEM(item.shape, item.dtype) for item in near],
         ],
         compiler_params=pltpu.CompilerParams(
-            collective_id=0, has_side_effects=True, vmem_limit_bytes=48 * 1024 * 1024
+            collective_id=0, has_side_effects=True, vmem_limit_bytes=63 * 1024 * 1024
         ),
         name="handover",
     )(
         places(m2g_src),
         places(mesh_src),
-        state,
-        mesh_latent,
-        local_ids,
-        lower_ids,
-        upper_ids,
-        norm_gain[:, None],
-        w_dec_mesh,
-        w_dec_grid,
-        w_dec_out.T,
-        w_enc,
-        w_enc_out,
-        w_proc_src,
-        w_proc_dst,
-        w_proc_out,
+        g2m_owner.T,
+        g2m_node.T,
+        norm_gain[None, :],
+        *near,
     )
 
 

time: 71.1 us -> 55.3 us (0.78)
  local copies, waits for them, and re-layouts: 13.7 us -> 6.33 us
  Pallas kernels: 53 us -> 46.1 us
  other arithmetic: 3.06 us -> 1.63 us
    unnamed x20 -> x2, local copies, waits for them, and re-layouts: 12.9 us -> 5.07 us
    pallas_call x1, Pallas kernels: 53 us -> 46.1 us  [shards(): pl.pallas_call(functools.partial(kernel, bands), out_shape=(jax.ShapeDtyp...]
    select_n x2 -> x0, other arithmetic: 1.44 us -> none  [the longest x1 0.73 us: shards(): local_ids = jnp.where(relative == 0, nodes, -1)]
    reshape x2, local copies, waits for them, and re-layouts: 0.04 us -> 1.26 us  [places(): return (4 * local + (PAD - 4 * parity)).reshape(-1)]
    broadcast_in_dim x1 -> x0, local copies, waits for them, and re-layouts: 0.76 us -> none  [shards(): norm_gain[:, None]]
where the time goes in v2:
time: 55.3 us; the launch traced here: 54.7 us
  Pallas kernels  46.1 us (83%)
  local copies, waits for them, and re-layouts  6.33 us (11%)
  other arithmetic  1.63 us (3%)
  between operations  0.65 us (1%)
    pallas_call x1, Pallas kernels, shards(): pl.pallas_call(functools.partial(kernel, bands), out_shape=(jax.ShapeDtyp...  46.1 us
    unnamed x2, local copies, waits for them, and re-layouts  5.07 us
    add x2, other arithmetic, places(): return (4 * local + (PAD - 4 * parity)).reshape(-1)  1.63 us
    reshape x2, local copies, waits for them, and re-layouts, places(): return (4 * local + (PAD - 4 * parity)).reshape(-1)  1.26 us

profile of v2, /device:TPU:1, one launch (start us, length us, event | category | flops | bytes accessed | tf_op | source)
XLA Modules:
  0.0 54.7 jit_solution(11807085214832508599)
XLA Ops:
  0.6 0.8 %add_bitcast_fusion.1 = s32[3,2048]{1,0:T(4,128)S(1)} fusion(s32[2048,3]{0,1:T(4,128)} %param.17, s32[2048]{0:T(1024)S(1)} %fusion.1, s32[]{:T(128)S(6)} %sub.29), kind=kLoop, calls=%fused_computation.1 | loop fusion | flops 18432 | bytes 57348 | tf_op jit(solution)/shard_map/add | solution.py:379
  1.4 0.6 %reshape.29.m2g_index = s32[6144]{0:T(1024)} reshape(s32[3,2048]{1,0:T(4,128)S(1)} %add_bitcast_fusion.1) | data formatting | bytes 49152 | tf_op jit(solution)/shard_map/reshape | solution.py:379
  2.0 0.9 %add_bitcast_fusion = s32[6,2048]{1,0:T(8,128)S(1)} fusion(s32[2048,6]{0,1:T(8,128)} %param.20, s32[2048]{0:T(1024)S(1)} %fusion.1, s32[]{:T(128)S(6)} %sub.29), kind=kLoop, calls=%fused_computation | loop fusion | flops 36864 | bytes 106500 | tf_op jit(solution)/shard_map/add | solution.py:379
  2.9 0.6 %reshape.30.mesh_index = s32[12288]{0:T(1024)} reshape(s32[6,2048]{1,0:T(8,128)S(1)} %add_bitcast_fusion) | data formatting | bytes 98304 | tf_op jit(solution)/shard_map/reshape | solution.py:379
  3.5 46.1 %handover.1 = (f32[83,2048]{1,0:T(8,128)}, bf16[2048,512]{1,0:T(8,128)(2,1)}) custom-call(s32[6144]{0:T(1024)} %reshape.29.m2g_index, s32[12288]{0:T(1024)} %reshape.30.mesh_index, s32[1,2048]{1,0:T(1,128)} %bitcast.9, s32[1,2048]{1,0:T(1,128)} %bitcast.10, f32[1,83]{1,0:T(1,128)} %bitcast.11, f32[83,2048]{1,0:T(8,128)} %far_state.1, ...), custom_call_target="tpu_custom_call" | custom-call | tf_op jit(solution)/shard_map/handover/pallas_call | solution.py:396
  49.6 2.0 %copy.19 = f32[83,2048]{1,0:T(8,128)} copy(f32[83,2048]{1,0:T(8,128)} %get-tuple-element.4) | data formatting | bytes 1359872
  51.6 3.0 %copy.20 = bf16[2048,512]{1,0:T(8,128)(2,1)} copy(bf16[2048,512]{1,0:T(8,128)(2,1)} %get-tuple-element.5) | data formatting | bytes 4194304
  (1 shorter events, 0.0 us)

commit v3 on v2

--- a/solution.py
+++ b/solution.py
@@ -37,13 +37,13 @@
     )
 
 
-def gather_sum(table, index, rows, fanout, base, total, first):
+def gather_sum(table, index, fanout, base, total, first):
     upper = lax.broadcasted_iota(jnp.int32, (8, 128), 0) >= 4
 
     def body(step, carry):
         point = pl.multiple_of(first + 2 * UNROLL * step, 2 * UNROLL)
         views = [
-            index.at[pl.ds(edge * rows + point, 2 * UNROLL)] for edge in range(fanout)
+            index.at[edge, 0, pl.ds(point, 2 * UNROLL)] for edge in range(fanout)
         ]
         near = base.at[pl.ds(pl.multiple_of(4 * point, 8 * UNROLL), 8 * UNROLL)]
         far = total.at[pl.ds(pl.multiple_of(step * 8 * UNROLL, 8 * UNROLL), 8 * UNROLL)]
@@ -69,8 +69,8 @@
 
 def kernel(
     bands,
-    m2g_index,
-    mesh_index,
+    m2g_src,
+    mesh_src,
     owner,
     node,
     gain_row,
@@ -100,6 +100,11 @@
     send_sem,
     recv_sem,
     load_sem,
+    index_sem,
+    m2g_place,
+    mesh_place,
+    m2g_index,
+    mesh_index,
     window_ids,
     local_ids,
     gain,
@@ -231,6 +236,18 @@
             rim[pl.ds(side * BLOCK, BLOCK), :] = jnp.zeros((BLOCK, rim.shape[1]), rim.dtype)
             rim_ids[side] = jnp.full((1, BLOCK), -1, jnp.int32)
 
+    parity = lax.broadcasted_iota(jnp.int32, (1, points), 1) % 2
+    shift = PAD - 4 * parity
+    span = rows + 2 * HALO
+    moves = []
+    for number, (sources, place, index) in enumerate(
+        ((m2g_src, m2g_place, m2g_index), (mesh_src, mesh_place, mesh_index))
+    ):
+        for edge in range(sources.shape[0]):
+            local = sources[edge : edge + 1, :] - (me * rows - HALO)
+            place[edge] = 4 * jnp.clip(local, 0, span - 1) + shift
+        moves.append(pltpu.make_async_copy(place, index, index_sem.at[number]))
+        moves[-1].start()
     relative = owner[...] - me
     local_ids[...] = jnp.where(relative == 0, node[...], -1)
     window_ids[0] = jnp.where(relative == -1, node[...], -1)[:, :BLOCK]
@@ -271,6 +288,8 @@
     lax.fori_loop(0, points // BLOCK, receive, 0)
     for name in ("w_dec_out", "w_enc"):
         loads[name].wait()
+    for move in moves:
+        move.wait()
     finish(proj_copy)
     unpack(halo_in)
 
@@ -279,7 +298,7 @@
         point = pl.multiple_of(block * BLOCK, BLOCK)
         columns = pl.ds(point, BLOCK)
         cells = state[:, columns]
-        gather_sum(table, m2g_index, points, KD, base, total, point)
+        gather_sum(table, m2g_index, KD, base, total, point)
         decoded = get_rows(total, 0, BLOCK).astype(jnp.bfloat16)
         fresh = cells + dot(w_dec_out[...], decoded, 1, 1)
         new_state[:, columns] = fresh
@@ -341,7 +360,7 @@
     def process(block, carry):
         row = pl.multiple_of(block * BLOCK, BLOCK)
         span = pl.ds(row, BLOCK)
-        gather_sum(table, mesh_index, rows, KN, base, total, row)
+        gather_sum(table, mesh_index, KN, base, total, row)
         edges = get_rows(total, 0, BLOCK).astype(jnp.bfloat16)
         result = middle[span, :].astype(jnp.float32) + dot(edges, w_proc_out[...])
         mesh_out[span, :] = result.astype(jnp.bfloat16)
@@ -368,18 +387,9 @@
     w_proc_dst,
     w_proc_out,
 ):
-    position = lax.axis_index("band")
     rows, width = mesh_latent.shape
     points = state.shape[1]
-
-    def places(sources):
-        count = sources.shape[0]
-        parity = lax.broadcasted_iota(jnp.int32, (1, count), 1) % 2
-        local = sources.T - (position * rows - HALO)
-        return (4 * local + (PAD - 4 * parity)).reshape(-1)
-
     vmem = pl.BlockSpec(memory_space=pltpu.VMEM)
-    smem = pl.BlockSpec(memory_space=pltpu.SMEM)
     hbm = pl.BlockSpec(memory_space=pltpu.HBM)
     near = (
         state,
@@ -396,10 +406,10 @@
     return pl.pallas_call(
         functools.partial(kernel, bands),
         out_shape=(
-            jax.ShapeDtypeStruct(state.shape, jnp.float32),
-            jax.ShapeDtypeStruct(mesh_latent.shape, jnp.bfloat16),
+            pltpu.VMEM(state.shape, jnp.float32),
+            pltpu.VMEM(mesh_latent.shape, jnp.bfloat16),
         ),
-        in_specs=[smem] * 2 + [vmem] * 3 + [hbm] * 10,
+        in_specs=[vmem] * 5 + [hbm] * 10,
         out_specs=(vmem, vmem),
         scratch_shapes=[
             pltpu.VMEM((PAD + 4 * (rows + 2 * HALO) + 8, 128), jnp.float32),
@@ -416,18 +426,23 @@
             pltpu.SemaphoreType.DMA((8,)),
             pltpu.SemaphoreType.DMA((8,)),
             pltpu.SemaphoreType.DMA((12,)),
+            pltpu.SemaphoreType.DMA((2,)),
+            pltpu.VMEM((KD, 1, points), jnp.int32),
+            pltpu.VMEM((KN, 1, rows), jnp.int32),
+            pltpu.SMEM((KD, 1, points), jnp.int32),
+            pltpu.SMEM((KN, 1, rows), jnp.int32),
             pltpu.VMEM((2, 1, BLOCK), jnp.int32),
             pltpu.VMEM((1, points), jnp.int32),
             pltpu.VMEM((state.shape[0], 1), jnp.float32),
             *[pltpu.VMEM(item.shape, item.dtype) for item in near],
         ],
         compiler_params=pltpu.CompilerParams(
-            collective_id=0, has_side_effects=True, vmem_limit_bytes=63 * 1024 * 1024
+            collective_id=0, has_side_effects=True, vmem_limit_bytes=60 * 1024 * 1024
         ),
         name="handover",
     )(
-        places(m2g_src),
-        places(mesh_src),
+        m2g_src.T,
+        mesh_src.T,
         g2m_owner.T,
         g2m_node.T,
         norm_gain[None, :],

time: 55.3 us -> 46.9 us (0.85)
  local copies, waits for them, and re-layouts: 6.33 us -> 2.18 us
  Pallas kernels: 46.1 us -> 43.7 us
  other arithmetic: 1.63 us -> 0 us
    unnamed x2, local copies, waits for them, and re-layouts: 5.07 us -> 2.18 us
    pallas_call x1, Pallas kernels: 46.1 us -> 43.7 us  [shards(): pl.pallas_call(functools.partial(kernel, bands), out_shape=(pltpu.VMEM(st...]
    add x2 -> x0, other arithmetic: 1.63 us -> none  [places(): return (4 * local + (PAD - 4 * parity)).reshape(-1)]
    reshape x2 -> x0, local copies, waits for them, and re-layouts: 1.26 us -> none  [places(): return (4 * local + (PAD - 4 * parity)).reshape(-1)]
where the time goes in v3:
time: 46.9 us; the launch traced here: 46.5 us
  Pallas kernels  43.7 us (93%)
  local copies, waits for them, and re-layouts  2.18 us (5%)
  between operations  0.64 us (1%)
    pallas_call x1, Pallas kernels, shards(): pl.pallas_call(functools.partial(kernel, bands), out_shape=(pltpu.VMEM(st...  43.7 us
    unnamed x2, local copies, waits for them, and re-layouts  2.18 us

profile of v3, /device:TPU:1, one launch (start us, length us, event | category | flops | bytes accessed | tf_op | source)
XLA Modules:
  0.0 46.5 jit_solution(6747799793426017693)
XLA Ops:
  0.6 43.7 %handover.1 = (f32[83,2048]{1,0:T(8,128)S(1)}, bf16[2048,512]{1,0:T(8,128)(2,1)S(1)}) custom-call(s32[3,2048]{1,0:T(4,128)} %bitcast.8, s32[6,2048]{1,0:T(8,128)} %bitcast.7, s32[1,2048]{1,0:T(1,128)} %bitcast.9, s32[1,2048]{1,0:T(1,128)} %bitcast.10, f32[1,83]{1,0:T(1,128)} %bitcast.11, f32[83,2048]{1,0:T(8,128)} %far_state.1, ...), custom_call_target="tpu_custom_call" | custom-call | tf_op jit(solution)/shard_map/handover/pallas_call | solution.py:406
  44.4 0.9 %copy.19 = f32[83,2048]{1,0:T(8,128)} copy(f32[83,2048]{1,0:T(8,128)S(1)} %get-tuple-element.2) | data formatting | bytes 1359872
  45.2 1.3 %copy.20 = bf16[2048,512]{1,0:T(8,128)(2,1)} copy(bf16[2048,512]{1,0:T(8,128)(2,1)S(1)} %get-tuple-element.3) | data formatting | bytes 4194304

commit v4 on v3

--- a/solution.py
+++ b/solution.py
@@ -10,8 +10,9 @@
 HALO = 128
 KD = 3
 KN = 6
-BLOCK = 256
-UNROLL = 16
+BLOCK = 512
+WINDOW = 256
+UNROLL = 32
 PAD = 8
 
 
@@ -143,9 +144,9 @@
         return copy(1, side, window_ids.at[side], rim_ids.at[1 - side])
 
     def rim_copy(side):
-        start = 0 if side == 0 else points - BLOCK
+        start = 0 if side == 0 else points - WINDOW
         return copy(
-            2, side, message.at[pl.ds(start, BLOCK)], rim.at[pl.ds((1 - side) * BLOCK, BLOCK)]
+            2, side, message.at[pl.ds(start, WINDOW)], rim.at[pl.ds((1 - side) * WINDOW, WINDOW)]
         )
 
     def start(make):
@@ -233,8 +234,8 @@
         def _():
             first = PAD + side * 4 * (HALO + rows)
             table[pl.ds(first, 4 * HALO), :] = jnp.zeros((4 * HALO, 128), jnp.float32)
-            rim[pl.ds(side * BLOCK, BLOCK), :] = jnp.zeros((BLOCK, rim.shape[1]), rim.dtype)
-            rim_ids[side] = jnp.full((1, BLOCK), -1, jnp.int32)
+            rim[pl.ds(side * WINDOW, WINDOW), :] = jnp.zeros((WINDOW, rim.shape[1]), rim.dtype)
+            rim_ids[side] = jnp.full((1, WINDOW), -1, jnp.int32)
 
     parity = lax.broadcasted_iota(jnp.int32, (1, points), 1) % 2
     shift = PAD - 4 * parity
@@ -250,8 +251,8 @@
         moves[-1].start()
     relative = owner[...] - me
     local_ids[...] = jnp.where(relative == 0, node[...], -1)
-    window_ids[0] = jnp.where(relative == -1, node[...], -1)[:, :BLOCK]
-    window_ids[1] = jnp.where(relative == 1, node[...], -1)[:, points - BLOCK :]
+    window_ids[0] = jnp.where(relative == -1, node[...], -1)[:, :WINDOW]
+    window_ids[1] = jnp.where(relative == 1, node[...], -1)[:, points - WINDOW :]
     start(ids_copy)
     channels = gain_row.shape[1]
     square = (channels, channels)
@@ -334,7 +335,7 @@
         span = pl.ds(row, BLOCK)
         encoded = collected[span, :]
         for side in (0, 1):
-            encoded += dot(one_hot(rim_ids[side], row), rim[pl.ds(side * BLOCK, BLOCK), :])
+            encoded += dot(one_hot(rim_ids[side], row), rim[pl.ds(side * WINDOW, WINDOW), :])
         mixed = latent[span, :].astype(jnp.float32) + dot(
             encoded.astype(jnp.bfloat16), w_enc_out[...]
         )
@@ -421,8 +422,8 @@
             pltpu.VMEM((2, 2, HALO, width), jnp.bfloat16),
             pltpu.VMEM((2, HALO, width), jnp.bfloat16),
             pltpu.VMEM((2, HALO, width), jnp.bfloat16),
-            pltpu.VMEM((2 * BLOCK, width), jnp.bfloat16),
-            pltpu.VMEM((2, 1, BLOCK), jnp.int32),
+            pltpu.VMEM((2 * WINDOW, width), jnp.bfloat16),
+            pltpu.VMEM((2, 1, WINDOW), jnp.int32),
             pltpu.SemaphoreType.DMA((8,)),
             pltpu.SemaphoreType.DMA((8,)),
             pltpu.SemaphoreType.DMA((12,)),
@@ -431,7 +432,7 @@
             pltpu.VMEM((KN, 1, rows), jnp.int32),
             pltpu.SMEM((KD, 1, points), jnp.int32),
             pltpu.SMEM((KN, 1, rows), jnp.int32),
-            pltpu.VMEM((2, 1, BLOCK), jnp.int32),
+            pltpu.VMEM((2, 1, WINDOW), jnp.int32),
             pltpu.VMEM((1, points), jnp.int32),
             pltpu.VMEM((state.shape[0], 1), jnp.float32),
             *[pltpu.VMEM(item.shape, item.dtype) for item in near],

time: 46.9 us -> 40.9 us (0.87)
  Pallas kernels: 43.7 us -> 37.9 us
    pallas_call x1, Pallas kernels: 43.7 us -> 37.9 us  [shards(): pl.pallas_call(functools.partial(kernel, bands), out_shape=(pltpu.VMEM(st...]
where the time goes in v4:
time: 40.9 us; the launch traced here: 40.7 us
  Pallas kernels  37.9 us (93%)
  local copies, waits for them, and re-layouts  2.18 us (5%)
  between operations  0.64 us (2%)
    pallas_call x1, Pallas kernels, shards(): pl.pallas_call(functools.partial(kernel, bands), out_shape=(pltpu.VMEM(st...  37.9 us
    unnamed x2, local copies, waits for them, and re-layouts  2.18 us

profile of v4, /device:TPU:1, one launch (start us, length us, event | category | flops | bytes accessed | tf_op | source)
XLA Modules:
  0.0 40.7 jit_solution(957035262674769094)
XLA Ops:
  0.6 37.9 %handover.1 = (f32[83,2048]{1,0:T(8,128)S(1)}, bf16[2048,512]{1,0:T(8,128)(2,1)S(1)}) custom-call(s32[3,2048]{1,0:T(4,128)} %bitcast.8, s32[6,2048]{1,0:T(8,128)} %bitcast.7, s32[1,2048]{1,0:T(1,128)} %bitcast.9, s32[1,2048]{1,0:T(1,128)} %bitcast.10, f32[1,83]{1,0:T(1,128)} %bitcast.11, f32[83,2048]{1,0:T(8,128)} %far_state.1, ...), custom_call_target="tpu_custom_call" | custom-call | tf_op jit(solution)/shard_map/handover/pallas_call | solution.py:407
  38.5 0.9 %copy.19 = f32[83,2048]{1,0:T(8,128)} copy(f32[83,2048]{1,0:T(8,128)S(1)} %get-tuple-element.2) | data formatting | bytes 1359872
  39.4 1.3 %copy.20 = bf16[2048,512]{1,0:T(8,128)(2,1)} copy(bf16[2048,512]{1,0:T(8,128)(2,1)S(1)} %get-tuple-element.3) | data formatting | bytes 4194304
